TPU v7x, 128 devices: a whole 4x4x4 slice. The times are simulated.
128 devices in a mesh: expert: 4 (over y), feat: 32 (over x, z, core).
Axes of the slice: x: 4, y: 4, z: 4, core: 2. Of those that a mesh axis runs over, the one named last changes fastest.
Arguments:
- tokens: bfloat16 [1024, 4096], P(('expert', 'feat')), may hold values from -6 to 6
- expert_ids: int32 [1024, 2], P(('expert', 'feat')), may hold values from 0 to 7, as said below
- route_weights: bfloat16 [1024, 2], P(('expert', 'feat')), may hold values from 0.099609375 to 1
- gate_proj: bfloat16 [4096, 28672], P(None, ('expert', 'feat')), may hold values from -0.09375 to 0.09375
- up_proj: bfloat16 [4096, 28672], P(None, ('expert', 'feat')), may hold values from -0.09375 to 0.09375
- down_proj: bfloat16 [28672, 4096], P(('expert', 'feat')), may hold values from -0.046875 to 0.046875
- enc_weight: float32 [4096, 32768], P(None, ('expert', 'feat')), may hold values from -0.09375 to 0.09375
- enc_bias: float32 [32768], P(('expert', 'feat')), may hold values from -3 to 3
- log_threshold: float32 [32768], P(('expert', 'feat')), may hold values from -2.3 to 0
- dec_weight: float32 [32768, 4096], P(('expert', 'feat')), may hold values from -0.046875 to 0.046875
Outputs:
- grad_encoder: float32 [4096, 32768], P(None, ('expert', 'feat'))
- grad_decoder: float32 [32768, 4096], P(('expert', 'feat'))
- grad_bias: float32 [32768], P(('expert', 'feat'))
- grad_threshold: float32 [32768], P(('expert', 'feat'))
Inputs may be any that keep to these rules, and one draw needn't show every extreme that they name: `expert_ids`: each token names two different experts of 0 to 7. Among the 8 tokens of one device, each expert below 2 is named by at most 4 tokens; in every draw one of these experts, drawn from the seed and the same for all devices, is named by exactly 4 tokens of every device.
All inputs are finite; a program needn't handle non-finite values.
Results may differ from a plain program's by a relative error of at most 0.0021.
Values may be sent and summed in bfloat16 or wider, within the bound.
A program may use at most 128 MiB of HBM per device.

v0:
```python
import jax
import jax.numpy as jnp
from jax import lax
from jax.sharding import PartitionSpec as P

sharpness = 0.1
kernel_width = 0.5
density_weight = 0.01


def partner(block, axis, stride):
    count = lax.axis_size(axis)
    route = []
    for low in range(count):
        high = low | 1 << stride
        if high != low and high < count:
            route += [(low, high), (high, low)]
    return lax.ppermute(block, axis, route)


def pack_slots(tokens, expert_ids, route_weights, experts):
    capacity = tokens.shape[0] // 2
    window = jnp.arange(experts, dtype=jnp.int32)
    matches = expert_ids[:, :, None] == window[None, None, :]
    named = jnp.sum(matches.astype(jnp.int32), axis=1)
    weighted = jnp.sum(
        jnp.where(matches, route_weights[:, :, None], jnp.zeros((), jnp.bfloat16)), axis=1
    )
    rows = jnp.arange(tokens.shape[0], dtype=jnp.int32)
    earlier = rows[None, :, None] < rows[:, None, None]
    slot_index = jnp.sum(jnp.where(earlier, named[None, :, :], 0), axis=1)
    places = jnp.arange(capacity, dtype=jnp.int32)
    chosen = (named.T[:, None, :] == 1) & (slot_index.T[:, None, :] == places[None, :, None])
    slot_rows = jnp.einsum(
        "ect,td->ecd", chosen.astype(jnp.bfloat16), tokens, preferred_element_type=jnp.float32
    ).astype(jnp.bfloat16)
    slot_weights = jnp.sum(
        jnp.where(chosen, weighted.T[:, None, :], jnp.zeros((), jnp.bfloat16)), axis=2
    )
    return (slot_rows, slot_weights)


def split(value):
    high = lax.reduce_precision(value, 8, 7)
    return (high.astype(jnp.bfloat16), (value - high).astype(jnp.bfloat16))


def product(left, right, dims):
    return lax.dot_general(left, right, (dims, ((), ())), preferred_element_type=jnp.float32)


def body(
    tokens,
    expert_ids,
    route_weights,
    gate_proj,
    up_proj,
    down_proj,
    enc_weight,
    enc_bias,
    log_threshold,
    dec_weight,
):
    copies = 2
    experts = lax.axis_size("expert") // copies
    slot_rows, slot_weights = pack_slots(tokens, expert_ids, route_weights, experts)
    send_rows = jnp.repeat(slot_rows, copies, axis=0)
    send_weights = jnp.repeat(slot_weights, copies, axis=0)
    came_rows, came_weights = (
        lax.all_to_all(send_rows, "expert", split_axis=0, concat_axis=0, tiled=True),
        lax.all_to_all(send_weights, "expert", split_axis=0, concat_axis=0, tiled=True),
    )
    all_rows, all_weights = (
        lax.all_gather(came_rows, "feat", axis=0, tiled=True),
        lax.all_gather(came_weights, "feat", axis=0, tiled=True),
    )
    width = tokens.shape[1]
    token_rows = all_rows.reshape(-1, width)
    row_weights = all_weights.reshape(-1).astype(jnp.float32)
    gate_act = jnp.dot(token_rows, gate_proj, preferred_element_type=jnp.float32)
    up_act = jnp.dot(token_rows, up_proj, preferred_element_type=jnp.float32)
    hidden = (jax.nn.silu(gate_act) * up_act).astype(jnp.bfloat16)
    target_part = jnp.dot(hidden, down_proj, preferred_element_type=jnp.float32)
    rows = ((1,), (0,))
    down = ((0,), (0,))
    enc_high, enc_low = split(enc_weight)
    dec_high, dec_low = split(dec_weight)
    preact = product(token_rows, enc_high, rows) + product(token_rows, enc_low, rows) + enc_bias
    threshold = jnp.exp(log_threshold)
    shifted = preact - threshold
    soft_gate = jax.nn.sigmoid(shifted / sharpness)
    active = preact * soft_gate
    act_high, act_low = split(active)
    recon = product(act_high, dec_high, rows) + product(act_high, dec_low, rows)
    partial_error = recon + product(act_low, dec_high, rows) - target_part
    feat_total = lax.psum_scatter(partial_error, "feat", scatter_dimension=0, tiled=True)
    recon_error = feat_total + partner(feat_total, "expert", 0)
    own_rows = feat_total.shape[0]
    own_weights = lax.dynamic_slice_in_dim(row_weights, lax.axis_index("feat") * own_rows, own_rows)
    own_grad = (2.0 * own_weights[:, None] * recon_error).astype(jnp.bfloat16)
    residual_grad = lax.all_gather(own_grad, "feat", axis=0, tiled=True)
    grad_decoder = product(act_high, residual_grad, down) + product(act_low, residual_grad, down)
    across = ((1,), (1,))
    grad_active = product(residual_grad, dec_high, across) + product(residual_grad, dec_low, across)
    grad_pre = grad_active * soft_gate
    pre_high, pre_low = split(grad_pre)
    grad_encoder = product(token_rows, pre_high, down) + product(token_rows, pre_low, down)
    grad_bias = jnp.sum(grad_pre, axis=0)
    kernel = jnp.maximum(0.0, 1.0 - jnp.abs(shifted) / kernel_width) / kernel_width
    slope_sum = jnp.sum(
        (grad_active * threshold + density_weight * row_weights[:, None]) * kernel, axis=0
    )
    grad_threshold = -threshold * slope_sum
    return (grad_encoder, grad_decoder, grad_bias, grad_threshold)


def solution(mesh):
    in_specs = (
        P(("expert", "feat"), None),
        P(("expert", "feat"), None),
        P(("expert", "feat"), None),
        P(None, ("expert", "feat")),
        P(None, ("expert", "feat")),
        P(("expert", "feat"), None),
        P(None, ("expert", "feat")),
        P(("expert", "feat")),
        P(("expert", "feat")),
        P(("expert", "feat"), None),
    )
    out_specs = (
        P(None, ("expert", "feat")),
        P(("expert", "feat"), None),
        P(("expert", "feat")),
        P(("expert", "feat")),
    )
    return jax.shard_map(body, mesh=mesh, in_specs=in_specs, out_specs=out_specs, check_vma=False)
```

profile of v0, /device:TPU:1, one launch (start us, length us, event | category | flops | bytes accessed | tf_op | source)
XLA Modules:
  0.0 313.5 jit_solution(17543353753348144969)
XLA Ops:
  7.2 0.0 copy-start
  7.2 0.0 all-gather.4.cloned.1.call-start
  7.2 0.8 convert_reduce_fusion.1
  8.1 0.1 select_reduce_fusion
  8.2 1.0 convolution_convert_fusion
  9.3 9.7 %all_to_all.17 = bf16[4,4,4096]{2,1,0:T(4,128)(2,1)} all-to-all(bf16[4,4,4096]{2,1,0:T(4,128)(2,1)S(1)} %bitcast.22), channel_id=1, replica_groups=mesh['expert'=4,'feat'=32] {'expert'}, dimensions={0} | all-to-all | bytes 262144 | tf_op jit(solution)/shard_map/all_to_all | solution.py:70
  19.0 0.0 all-gather.4.cloned.1.call-update
  19.0 0.0 reduce-scatter.2.cloned.1.call-start
  19.1 0.7 exp.10
  19.8 48.0 %all-gather.4.cloned.1.call-done = bf16[128,4,4096]{2,1,0:T(4,128)(2,1)} async-done(((bf16[4,4,4096]{2,1,0:T(4,128)(2,1)}), bf16[128,4,4096]{2,1,0:T(4,128)(2,1)}) %all-gather.4.cloned.1.call-update) | async-done | bytes 4194320 | tf_op jit(solution)/shard_map/all_gather | solution.py:74
  67.8 6.9 %reshape.55 = bf16[512,4096]{1,0:T(8,128)(2,1)} reshape(bf16[128,4,4096]{2,1,0:T(4,128)(2,1)} %all-gather.4.cloned.1.call-done) | data formatting | bytes 8388608 | tf_op jit(solution)/shard_map/reshape | solution.py:78
  74.6 4.9 %fusion.2 = f32[512,256]{1,0:T(8,128)S(1)} fusion(bf16[512,4096]{1,0:T(8,128)(2,1)} %reshape.55, f32[4096,256]{1,0:T(8,128)} %param.16), kind=kOutput, calls=%fused_computation.10 | convolution fusion | flops 1076887552 | bytes 8912896 | tf_op jit(solution)/shard_map/dot_general | solution.py:49
  79.5 0.0 copy-done.2
  79.5 1.0 copy-done.7
  80.6 0.0 copy-done.8
  80.6 1.3 fusion.6
  81.8 0.9 copy-done.5
  82.8 4.6 %fusion.11 = f32[512,4096]{1,0:T(8,128)} fusion(f32[256,4096]{1,0:T(8,128)S(1)} %copy-done.5, f32[512,256]{1,0:T(8,128)S(1)} %fusion.6, f32[256]{0:T(256)S(1)} %exp.10), kind=kOutput, calls=%fused_computation.23 | convolution fusion | flops 1077936128 | bytes 13108224 | tf_op jit(solution)/shard_map/dot_general | solution.py:49
  87.3 4.5 %fusion.38 = f32[512,4096]{1,0:T(8,128)} fusion(f32[256,4096]{1,0:T(8,128)S(1)} %copy-done.5, f32[512,256]{1,0:T(8,128)S(1)} %fusion.6, f32[256]{0:T(256)S(1)} %exp.10), kind=kOutput, calls=%fused_computation.58 | convolution fusion | flops 1076887552 | bytes 13108224 | tf_op jit(solution)/shard_map/dot_general | solution.py:49
  91.9 0.0 copy-done.12
  91.9 1.4 fusion.46
  93.3 8.7 %fusion.8 = f32[512,4096]{1,0:T(8,128)} fusion(bf16[224,4096]{1,0:T(8,128)(2,1)S(1)} %copy-done, bf16[512,4096]{1,0:T(8,128)(2,1)} %reshape.55, bf16[4096,224]{0,1:T(8,128)(2,1)} %param.14, f32[512,224]{0,1:T(8,128)S(1)} %fusion.46), kind=kOutput, calls=%fused_computation.17 | convolution fusion | flops 1879736320 | bytes 16711680 | tf_op jit(solution)/shard_map/dot_general | solution.py:83
  102.0 14.3 %add_subtract_fusion = f32[512,4096]{1,0:T(8,128)} fusion(f32[512,4096]{1,0:T(8,128)} %fusion.8, f32[512,4096]{1,0:T(8,128)} %fusion.38, f32[512,4096]{1,0:T(8,128)} %fusion.11, f32[256,4096]{1,0:T(8,128)} %param.19, f32[512,256]{1,0:T(8,128)S(1)} %fusion.6, f32[256]{0:T(256)S(1)} %exp.10), kind=kOutput, calls=%fused_computation | convolution fusion | flops 1083310080 | bytes 38274048 | tf_op jit(solution)/shard_map/dot_general | solution.py:49
  116.3 0.0 reduce-scatter.2.cloned.1.call-update
  116.3 0.7 copy-done.10
  117.0 89.5 %reduce-scatter.2.cloned.1.call-done = f32[16,4096]{1,0:T(8,128)} async-done(((f32[512,4096]{1,0:T(8,128)}), f32[16,4096]{1,0:T(8,128)}) %reduce-scatter.2.cloned.1.call-update) | async-done | bytes 262160 | tf_op jit(solution)/shard_map/reduce_scatter | solution.py:96
  206.5 1.2 collective-permute-start
  207.7 0.1 fusion.32
  207.8 0.6 copy.24
  208.4 3.7 %all-to-all-start.1 = ((bf16[4,1,4]{2,1,0:T(2,128)(2,1)}), bf16[4,1,4]{2,1,0:T(2,128)(2,1)S(1)}, u32[]{:S(2)}, u32[]{:S(2)}) async-start(bf16[4,1,4]{2,1,0:T(2,128)(2,1)} %copy.24), calls=%async_computation.1 | async-start | bytes 4096 | tf_op jit(solution)/shard_map/all_to_all | solution.py:71
  212.1 4.1 %all-to-all-done.1 = bf16[4,1,4]{2,1,0:T(2,128)(2,1)S(1)} async-done(((bf16[4,1,4]{2,1,0:T(2,128)(2,1)}), bf16[4,1,4]{2,1,0:T(2,128)(2,1)S(1)}, u32[]{:S(2)}, u32[]{:S(2)}) %all-to-all-start.1) | async-done | bytes 64 | tf_op jit(solution)/shard_map/all_to_all | solution.py:71
  216.2 27.5 %all-gather = bf16[128,1,4]{2,1,0:T(2,128)(2,1)S(1)} all-gather(bf16[4,1,4]{2,1,0:T(2,128)(2,1)S(1)} %all-to-all-done.1), channel_id=2, replica_groups=mesh['expert'=4,'feat'=32] {'feat'}, dimensions={0}, use_global_device_ids=true | all-gather | bytes 1056 | tf_op jit(solution)/shard_map/all_gather | solution.py:75
  243.7 0.2 convert_reduce_fusion
  243.9 0.1 reshape.56
  244.0 0.1 dynamic-slice_multiply_fusion
  244.1 0.0 collective-permute-done
  244.1 1.7 multiply_convert_fusion
  245.8 0.0 all-gather.6.cloned.1.call-update
  245.8 43.2 %all-gather.6.cloned.1.call-done = bf16[512,4096]{1,0:T(8,128)(2,1)} async-done(((bf16[16,4096]{1,0:T(8,128)(2,1)}), bf16[512,4096]{1,0:T(8,128)(2,1)}) %all-gather.6.cloned.1.call-update) | async-done | bytes 4194320 | tf_op jit(solution)/shard_map/all_gather | solution.py:101
  289.0 4.9 %fusion.9 = f32[512,256]{1,0:T(8,128)S(1)} fusion(bf16[512,4096]{1,0:T(8,128)(2,1)} %all-gather.6.cloned.1.call-done, f32[256,4096]{1,0:T(8,128)} %param.19), kind=kOutput, calls=%fused_computation.22 | convolution fusion | flops 1076887552 | bytes 8912896 | tf_op jit(solution)/shard_map/dot_general | solution.py:49
  293.9 1.0 copy-done.6
  294.9 2.0 fusion.44
  296.9 0.6 negate_multiply_fusion
  297.5 1.3 fusion.23
  298.8 3.3 %convolution_add_fusion.1 = f32[4096,256]{1,0:T(8,128)} fusion(f32[4096,256]{1,0:T(8,128)S(1)} %fusion.23, bf16[512,4096]{1,0:T(8,128)(2,1)S(1)} %copy-done.3, f32[512,256]{1,0:T(8,128)S(1)} %get-tuple-element.5), kind=kOutput, calls=%fused_computation.6 | convolution fusion | flops 1075183616 | bytes 13107200 | tf_op jit(solution)/shard_map/dot_general | solution.py:49
  302.1 1.4 fusion.25
  303.5 3.5 %convolution_add_fusion = f32[256,4096]{1,0:T(8,128)} fusion(f32[256,4096]{1,0:T(8,128)S(1)} %fusion.25, bf16[512,4096]{1,0:T(8,128)(2,1)S(1)} %copy-done.4, f32[512,256]{1,0:T(8,128)S(1)} %fusion.6, f32[256]{0:T(256)S(1)} %exp.10), kind=kOutput, calls=%fused_computation.5 | convolution fusion | flops 1075838976 | bytes 13108224 | tf_op jit(solution)/shard_map/dot_general | solution.py:49
  307.0 0.0 copy-done.1
  (24 shorter events, 0.1 us)
Async XLA Ops:
  7.2 86.1 %copy-start = (bf16[224,4096]{1,0:T(8,128)(2,1)S(1)}, bf16[224,4096]{1,0:T(8,128)(2,1)}, u32[]{:S(2)}) copy-start(bf16[224,4096]{1,0:T(8,128)(2,1)} %param.15) | copy-start | bytes 5505028
  7.2 60.6 %all-gather.4.cloned.1.call-start = ((), (), s32[]{:S(2)}) async-start(), calls=%async_computation.3 | async-start | bytes 4325376 | tf_op jit(solution)/shard_map/all_gather | solution.py:74
  19.0 187.5 %reduce-scatter.2.cloned.1.call-start = ((), (), s32[]{:S(2)}) async-start(), calls=%async_computation.4 | async-start | bytes 8650752 | tf_op jit(solution)/shard_map/reduce_scatter | solution.py:96
  74.6 4.9 %copy-start.2 = (bf16[512,4096]{1,0:T(8,128)(2,1)S(1)}, bf16[512,4096]{1,0:T(8,128)(2,1)}, u32[]{:S(2)}) copy-start(bf16[512,4096]{1,0:T(8,128)(2,1)} %reshape.55) | copy-start | bytes 12582916
  74.6 5.9 %copy-start.7 = (f32[4096,256]{1,0:T(8,128)S(1)}, f32[4096,256]{1,0:T(8,128)}, u32[]{:S(2)}) copy-start(f32[4096,256]{1,0:T(8,128)} %param.16) | copy-start | bytes 12582916
  74.6 5.9 %copy-start.8 = (f32[256]{0:T(256)S(1)}, f32[256]{0:T(256)}, u32[]{:S(2)}) copy-start(f32[256]{0:T(256)} %param.17) | copy-start | bytes 3076
  80.6 2.2 copy-start.5
  87.3 4.5 %copy-start.12 = (bf16[4096,224]{0,1:T(8,128)(2,1)S(1)}, bf16[4096,224]{0,1:T(8,128)(2,1)}, u32[]{:S(2)}) copy-start(bf16[4096,224]{0,1:T(8,128)(2,1)} %param.13) | copy-start | bytes 5505028
  116.3 0.7 copy-start.10
  116.3 0.7 copy-start.11
  206.5 37.6 %collective-permute-start = (f32[16,4096]{1,0:T(8,128)}, f32[16,4096]{1,0:T(8,128)S(1)}, u32[]{:S(2)}, u32[]{:S(2)}) collective-permute-start(f32[16,4096]{1,0:T(8,128)} %reduce-scatter.2.cloned.1.call-done), channel_id=1, source_target_pairs={{0,32},{32,0},{64,96},{96,64},{1,33},{33,1},{65,97},{97,65},{2,34}... | collective-permute-start | bytes 786440 | tf_op jit(solution)/shard_map/ppermute | solution.py:18
  208.4 7.8 %all-to-all-start.1 = ((bf16[4,1,4]{2,1,0:T(2,128)(2,1)}), bf16[4,1,4]{2,1,0:T(2,128)(2,1)S(1)}, u32[]{:S(2)}, u32[]{:S(2)}) async-start(bf16[4,1,4]{2,1,0:T(2,128)(2,1)} %copy.24), calls=%async_computation.1 | async-start | bytes 4096 | tf_op jit(solution)/shard_map/all_to_all | solution.py:71
  212.1 76.9 %all-gather.6.cloned.1.call-start = ((), (), s32[]{:S(2)}) async-start(), calls=%async_computation.5 | async-start | bytes 4325376 | tf_op jit(solution)/shard_map/all_gather | solution.py:101
  289.0 4.9 %copy-start.4 = (bf16[512,4096]{1,0:T(8,128)(2,1)S(1)}, bf16[512,4096]{1,0:T(8,128)(2,1)}, u32[]{:S(2)}) copy-start(bf16[512,4096]{1,0:T(8,128)(2,1)} %all-gather.6.cloned.1.call-done) | copy-start | bytes 12582916
  289.0 5.9 %copy-start.6 = (f32[256,4096]{1,0:T(8,128)S(1)}, f32[256,4096]{1,0:T(8,128)}, u32[]{:S(2)}) copy-start(f32[256,4096]{1,0:T(8,128)} %param.19) | copy-start | bytes 12582916
  294.9 2.0 copy-start.9
  294.9 2.6 copy-start.3
  302.1 4.9 %copy-start.1 = (bf16[224,4096]{1,0:T(8,128)(2,1)S(1)}, bf16[224,4096]{1,0:T(8,128)(2,1)}, u32[]{:S(2)}) copy-start(bf16[224,4096]{1,0:T(8,128)(2,1)} %param.15) | copy-start | bytes 5505028
Sparse Core Ops, SparseCore 0:
  19.1 48.5 all-gather.3
  116.5 89.9 reduce-scatter.1
  245.9 43.0 all-gather.5
where the time goes:
time: 314 us
  waiting for transfers between devices  185 us (59%)
  matrix products  57.1 us (18%)
  blocking collectives  37.3 us (12%)
  between operations  13.9 us (4%)
  local copies, waits for them, and re-layouts  11.9 us (4%)
  starting transfers between devices  4.98 us (2%)
  other arithmetic  3.61 us (1%)
    reduce_scatter x1, waiting for transfers between devices, body(): lax.psum_scatter(partial_error, 'feat', scatter_dimension=0, tiled=True)  89.5 us
    all_gather x1, waiting for transfers between devices, body(): lax.all_gather(came_rows, 'feat', axis=0, tiled=True)  48 us
    dot_general x11, matrix products, product(): lax.dot_general(left, right, (dims, ((), ())), preferred_element_type=jnp...  45.9 us
    all_gather x1, waiting for transfers between devices, body(): residual_grad = lax.all_gather(own_grad, 'feat', axis=0, tiled=True)  43.2 us
    all_gather x1, blocking collectives, body(): lax.all_gather(came_weights, 'feat', axis=0, tiled=True)  27.5 us
    all_to_all x1, blocking collectives, body(): lax.all_to_all(send_rows, 'expert', split_axis=0, concat_axis=0, tiled=True)  9.75 us
    dot_general x1, matrix products, body(): target_part = jnp.dot(hidden, down_proj, preferred_element_type=jnp.float32)  8.72 us
    reshape x1, local copies, waits for them, and re-layouts, body(): token_rows = all_rows.reshape(-1, width)  6.87 us
  transfers between devices with their start and end apart: 5, of which 4 were waited for; matrix products, arithmetic and copies ran while one was open for 1% of the time, Pallas kernels for 0%

commit v1 on v0

--- a/solution.py
+++ b/solution.py
@@ -72,7 +72,9 @@
     )
     all_rows, all_weights = (
         lax.all_gather(came_rows, "feat", axis=0, tiled=True),
-        lax.all_gather(came_weights, "feat", axis=0, tiled=True),
+        jnp.concatenate(
+            lax.all_to_all(jnp.stack([came_weights] * lax.axis_size("feat")), "feat", 0, 0), axis=0
+        ),
     )
     width = tokens.shape[1]
     token_rows = all_rows.reshape(-1, width)

time: 314 us -> 302 us (0.962)
  blocking collectives: 37.3 us -> 17.4 us
  starting transfers between devices: 4.98 us -> 10.5 us
    all_gather x1 -> x0, blocking collectives: 27.5 us -> none  [body(): lax.all_gather(came_weights, 'feat', axis=0, tiled=True)]
    all_to_all x0 -> x1, blocking collectives: none -> 7.67 us  [body(): lax.all_to_all(send_weights, 'expert', split_axis=0, concat_axis=0, tiled...]
    all_to_all x1, starting transfers between devices: 3.71 us -> 8.95 us  [body(): lax.all_to_all(jnp.stack([came_weights] * lax.axis_size('feat')), 'feat',...]
where the time goes in v1:
time: 302 us; the launch traced here: 301 us
  waiting for transfers between devices  188 us (62%)
  matrix products  57.1 us (19%)
  blocking collectives  17.4 us (6%)
  between operations  13.9 us (5%)
  local copies, waits for them, and re-layouts  11.3 us (4%)
  starting transfers between devices  10.5 us (3%)
  other arithmetic  3.42 us (1%)
    reduce_scatter x1, waiting for transfers between devices, body(): lax.psum_scatter(partial_error, 'feat', scatter_dimension=0, tiled=True)  90.1 us
    all_gather x1, waiting for transfers between devices, body(): lax.all_gather(came_rows, 'feat', axis=0, tiled=True)  48 us
    dot_general x11, matrix products, product(): lax.dot_general(left, right, (dims, ((), ())), preferred_element_type=jnp...  45.9 us
    all_gather x1, waiting for transfers between devices, body(): residual_grad = lax.all_gather(own_grad, 'feat', axis=0, tiled=True)  42.4 us
    all_to_all x1, blocking collectives, body(): lax.all_to_all(send_rows, 'expert', split_axis=0, concat_axis=0, tiled=True)  9.75 us
    all_to_all x1, starting transfers between devices, body(): lax.all_to_all(jnp.stack([came_weights] * lax.axis_size('feat')), 'feat',...  8.95 us
    dot_general x1, matrix products, body(): target_part = jnp.dot(hidden, down_proj, preferred_element_type=jnp.float32)  8.71 us
    all_to_all x1, blocking collectives, body(): lax.all_to_all(send_weights, 'expert', split_axis=0, concat_axis=0, tiled...  7.67 us
  transfers between devices with their start and end apart: 5, of which 4 were waited for; matrix products, arithmetic and copies ran while one was open for 1% of the time, Pallas kernels for 0%

profile of v1, /device:TPU:1, one launch (start us, length us, event | category | flops | bytes accessed | tf_op | source)
XLA Modules:
  0.0 301.2 jit_solution(10796201367737204666)
XLA Ops:
  7.2 0.0 copy-start
  7.2 0.0 all-gather.3.cloned.1.call-start
  7.2 0.8 convert_reduce_fusion
  8.1 0.1 select_reduce_fusion
  8.2 1.0 convolution_convert_fusion
  9.3 9.7 %all_to_all.19 = bf16[4,4,4096]{2,1,0:T(4,128)(2,1)} all-to-all(bf16[4,4,4096]{2,1,0:T(4,128)(2,1)S(1)} %bitcast.25), channel_id=1, replica_groups=mesh['expert'=4,'feat'=32] {'expert'}, dimensions={0} | all-to-all | bytes 262144 | tf_op jit(solution)/shard_map/all_to_all | solution.py:70
  19.0 0.0 all-gather.3.cloned.1.call-update
  19.0 0.0 reduce-scatter.2.cloned.1.call-start
  19.1 0.7 exp.10
  19.8 48.0 %all-gather.3.cloned.1.call-done = bf16[128,4,4096]{2,1,0:T(4,128)(2,1)} async-done(((bf16[4,4,4096]{2,1,0:T(4,128)(2,1)}), bf16[128,4,4096]{2,1,0:T(4,128)(2,1)}) %all-gather.3.cloned.1.call-update) | async-done | bytes 4194320 | tf_op jit(solution)/shard_map/all_gather | solution.py:74
  67.8 6.9 %reshape.57 = bf16[512,4096]{1,0:T(8,128)(2,1)} reshape(bf16[128,4,4096]{2,1,0:T(4,128)(2,1)} %all-gather.3.cloned.1.call-done) | data formatting | bytes 8388608 | tf_op jit(solution)/shard_map/reshape | solution.py:80
  74.6 4.9 %fusion.2 = f32[512,256]{1,0:T(8,128)S(1)} fusion(bf16[512,4096]{1,0:T(8,128)(2,1)} %reshape.57, f32[4096,256]{1,0:T(8,128)} %param.16), kind=kOutput, calls=%fused_computation.10 | convolution fusion | flops 1076887552 | bytes 8912896 | tf_op jit(solution)/shard_map/dot_general | solution.py:49
  79.5 0.0 copy-done.2
  79.5 1.0 copy-done.7
  80.6 0.0 copy-done.8
  80.6 1.3 fusion.6
  81.8 0.9 copy-done.5
  82.8 4.6 %fusion.11 = f32[512,4096]{1,0:T(8,128)} fusion(f32[256,4096]{1,0:T(8,128)S(1)} %copy-done.5, f32[512,256]{1,0:T(8,128)S(1)} %fusion.6, f32[256]{0:T(256)S(1)} %exp.10), kind=kOutput, calls=%fused_computation.23 | convolution fusion | flops 1077936128 | bytes 13108224 | tf_op jit(solution)/shard_map/dot_general | solution.py:49
  87.3 4.5 %fusion.38 = f32[512,4096]{1,0:T(8,128)} fusion(f32[256,4096]{1,0:T(8,128)S(1)} %copy-done.5, f32[512,256]{1,0:T(8,128)S(1)} %fusion.6, f32[256]{0:T(256)S(1)} %exp.10), kind=kOutput, calls=%fused_computation.58 | convolution fusion | flops 1076887552 | bytes 13108224 | tf_op jit(solution)/shard_map/dot_general | solution.py:49
  91.8 0.0 copy-done.12
  91.8 1.4 fusion.46
  93.3 0.0 copy-done
  93.3 8.7 %fusion.8 = f32[512,4096]{1,0:T(8,128)} fusion(bf16[224,4096]{1,0:T(8,128)(2,1)S(1)} %copy-done, bf16[512,4096]{1,0:T(8,128)(2,1)} %reshape.57, bf16[4096,224]{0,1:T(8,128)(2,1)} %param.14, f32[512,224]{0,1:T(8,128)S(1)} %fusion.46), kind=kOutput, calls=%fused_computation.17 | convolution fusion | flops 1879736320 | bytes 16711680 | tf_op jit(solution)/shard_map/dot_general | solution.py:85
  102.0 14.3 %add_subtract_fusion = f32[512,4096]{1,0:T(8,128)} fusion(f32[512,4096]{1,0:T(8,128)} %fusion.8, f32[512,4096]{1,0:T(8,128)} %fusion.38, f32[512,4096]{1,0:T(8,128)} %fusion.11, f32[256,4096]{1,0:T(8,128)} %param.19, f32[512,256]{1,0:T(8,128)S(1)} %fusion.6, f32[256]{0:T(256)S(1)} %exp.10), kind=kOutput, calls=%fused_computation | convolution fusion | flops 1083310080 | bytes 38274048 | tf_op jit(solution)/shard_map/dot_general | solution.py:49
  116.3 0.0 reduce-scatter.2.cloned.1.call-update
  116.3 90.1 %reduce-scatter.2.cloned.1.call-done = f32[16,4096]{1,0:T(8,128)} async-done(((f32[512,4096]{1,0:T(8,128)}), f32[16,4096]{1,0:T(8,128)}) %reduce-scatter.2.cloned.1.call-update) | async-done | bytes 262160 | tf_op jit(solution)/shard_map/reduce_scatter | solution.py:98
  206.5 1.2 collective-permute-start
  207.7 0.0 copy-done.11
  207.7 0.1 fusion.32
  207.8 7.7 %all_to_all.20 = bf16[4,1,4]{2,1,0:T(2,128)(2,1)S(1)} all-to-all(bf16[4,1,4]{2,1,0:T(2,128)(2,1)S(1)} %copy.28), channel_id=1, replica_groups=mesh['expert'=4,'feat'=32] {'expert'}, dimensions={0} | all-to-all | bytes 64 | tf_op jit(solution)/shard_map/all_to_all | solution.py:71
  215.5 0.6 stack.5
  216.1 9.0 %all-to-all-start.2 = ((bf16[32,4,4]{2,1,0:T(4,128)(2,1)}), bf16[32,4,4]{2,1,0:T(4,128)(2,1)S(1)}, u32[]{:S(2)}, u32[]{:S(2)}) async-start(bf16[32,4,4]{2,1,0:T(4,128)(2,1)} %stack.5), calls=%async_computation.2 | async-start | bytes 65536 | tf_op jit(solution)/shard_map/all_to_all | solution.py:76
  225.1 0.2 all-gather.5.cloned.1.call-start
  225.3 7.0 %all-to-all-done.2 = bf16[32,4,4]{2,1,0:T(4,128)(2,1)S(1)} async-done(((bf16[32,4,4]{2,1,0:T(4,128)(2,1)}), bf16[32,4,4]{2,1,0:T(4,128)(2,1)S(1)}, u32[]{:S(2)}, u32[]{:S(2)}) %all-to-all-start.2) | async-done | bytes 1056 | tf_op jit(solution)/shard_map/all_to_all | solution.py:76
  232.4 0.1 reshape.58
  232.5 0.1 dynamic-slice_multiply_fusion
  232.6 0.0 collective-permute-done
  232.6 1.7 multiply_convert_fusion
  234.3 0.0 all-gather.5.cloned.1.call-update
  234.3 42.4 %all-gather.5.cloned.1.call-done = bf16[512,4096]{1,0:T(8,128)(2,1)} async-done(((bf16[16,4096]{1,0:T(8,128)(2,1)}), bf16[512,4096]{1,0:T(8,128)(2,1)}) %all-gather.5.cloned.1.call-update) | async-done | bytes 4194320 | tf_op jit(solution)/shard_map/all_gather | solution.py:103
  276.7 4.9 %fusion.9 = f32[512,256]{1,0:T(8,128)S(1)} fusion(bf16[512,4096]{1,0:T(8,128)(2,1)} %all-gather.5.cloned.1.call-done, f32[256,4096]{1,0:T(8,128)} %param.19), kind=kOutput, calls=%fused_computation.22 | convolution fusion | flops 1076887552 | bytes 8912896 | tf_op jit(solution)/shard_map/dot_general | solution.py:49
  281.6 1.0 copy-done.6
  282.6 2.0 fusion.44
  284.6 0.6 negate_multiply_fusion
  285.2 1.3 fusion.23
  286.5 3.3 %convolution_add_fusion.1 = f32[4096,256]{1,0:T(8,128)} fusion(f32[4096,256]{1,0:T(8,128)S(1)} %fusion.23, bf16[512,4096]{1,0:T(8,128)(2,1)S(1)} %copy-done.3, f32[512,256]{1,0:T(8,128)S(1)} %get-tuple-element.5), kind=kOutput, calls=%fused_computation.6 | convolution fusion | flops 1075183616 | bytes 13107200 | tf_op jit(solution)/shard_map/dot_general | solution.py:49
  289.8 1.4 fusion.25
  291.2 3.5 %convolution_add_fusion = f32[256,4096]{1,0:T(8,128)} fusion(f32[256,4096]{1,0:T(8,128)S(1)} %fusion.25, bf16[512,4096]{1,0:T(8,128)(2,1)S(1)} %copy-done.4, f32[512,256]{1,0:T(8,128)S(1)} %fusion.6, f32[256]{0:T(256)S(1)} %exp.10), kind=kOutput, calls=%fused_computation.5 | convolution fusion | flops 1075838976 | bytes 13108224 | tf_op jit(solution)/shard_map/dot_general | solution.py:49
  (25 shorter events, 0.1 us)
Async XLA Ops:
  7.2 86.1 %copy-start = (bf16[224,4096]{1,0:T(8,128)(2,1)S(1)}, bf16[224,4096]{1,0:T(8,128)(2,1)}, u32[]{:S(2)}) copy-start(bf16[224,4096]{1,0:T(8,128)(2,1)} %param.15) | copy-start | bytes 5505028
  7.2 60.6 %all-gather.3.cloned.1.call-start = ((), (), s32[]{:S(2)}) async-start(), calls=%async_computation.4 | async-start | bytes 4325376 | tf_op jit(solution)/shard_map/all_gather | solution.py:74
  19.0 187.5 %reduce-scatter.2.cloned.1.call-start = ((), (), s32[]{:S(2)}) async-start(), calls=%async_computation.5 | async-start | bytes 8650752 | tf_op jit(solution)/shard_map/reduce_scatter | solution.py:98
  74.6 4.9 %copy-start.2 = (bf16[512,4096]{1,0:T(8,128)(2,1)S(1)}, bf16[512,4096]{1,0:T(8,128)(2,1)}, u32[]{:S(2)}) copy-start(bf16[512,4096]{1,0:T(8,128)(2,1)} %reshape.57) | copy-start | bytes 12582916
  74.6 5.9 %copy-start.7 = (f32[4096,256]{1,0:T(8,128)S(1)}, f32[4096,256]{1,0:T(8,128)}, u32[]{:S(2)}) copy-start(f32[4096,256]{1,0:T(8,128)} %param.16) | copy-start | bytes 12582916
  74.6 5.9 %copy-start.8 = (f32[256]{0:T(256)S(1)}, f32[256]{0:T(256)}, u32[]{:S(2)}) copy-start(f32[256]{0:T(256)} %param.17) | copy-start | bytes 3076
  80.6 2.2 copy-start.5
  87.3 4.5 %copy-start.12 = (bf16[4096,224]{0,1:T(8,128)(2,1)S(1)}, bf16[4096,224]{0,1:T(8,128)(2,1)}, u32[]{:S(2)}) copy-start(bf16[4096,224]{0,1:T(8,128)(2,1)} %param.13) | copy-start | bytes 5505028
  116.3 91.4 %copy-start.10 = (s32[8,2]{0,1:T(2,128)S(1)}, s32[8,2]{0,1:T(2,128)}, u32[]{:S(2)}) copy-start(s32[8,2]{0,1:T(2,128)} %param.11) | copy-start | bytes 196
  116.3 91.4 %copy-start.11 = (bf16[8,2]{0,1:T(2,128)(2,1)S(1)}, bf16[8,2]{0,1:T(2,128)(2,1)}, u32[]{:S(2)}) copy-start(bf16[8,2]{0,1:T(2,128)(2,1)} %param.12) | copy-start | bytes 100
  206.5 26.1 %collective-permute-start = (f32[16,4096]{1,0:T(8,128)}, f32[16,4096]{1,0:T(8,128)S(1)}, u32[]{:S(2)}, u32[]{:S(2)}) collective-permute-start(f32[16,4096]{1,0:T(8,128)} %reduce-scatter.2.cloned.1.call-done), channel_id=1, source_target_pairs={{0,32},{32,0},{64,96},{96,64},{1,33},{33,1},{65,97},{97,65},{2,34}... | collective-permute-start | bytes 786440 | tf_op jit(solution)/shard_map/ppermute | solution.py:18
  216.1 16.2 %all-to-all-start.2 = ((bf16[32,4,4]{2,1,0:T(4,128)(2,1)}), bf16[32,4,4]{2,1,0:T(4,128)(2,1)S(1)}, u32[]{:S(2)}, u32[]{:S(2)}) async-start(bf16[32,4,4]{2,1,0:T(4,128)(2,1)} %stack.5), calls=%async_computation.2 | async-start | bytes 65536 | tf_op jit(solution)/shard_map/all_to_all | solution.py:76
  225.1 51.6 %all-gather.5.cloned.1.call-start = ((), (), s32[]{:S(2)}) async-start(), calls=%async_computation.6 | async-start | bytes 4325376 | tf_op jit(solution)/shard_map/all_gather | solution.py:103
  276.7 4.9 %copy-start.4 = (bf16[512,4096]{1,0:T(8,128)(2,1)S(1)}, bf16[512,4096]{1,0:T(8,128)(2,1)}, u32[]{:S(2)}) copy-start(bf16[512,4096]{1,0:T(8,128)(2,1)} %all-gather.5.cloned.1.call-done) | copy-start | bytes 12582916
  276.7 5.9 %copy-start.6 = (f32[256,4096]{1,0:T(8,128)S(1)}, f32[256,4096]{1,0:T(8,128)}, u32[]{:S(2)}) copy-start(f32[256,4096]{1,0:T(8,128)} %param.19) | copy-start | bytes 12582916
  282.6 2.0 copy-start.9
  282.6 2.6 copy-start.3
  289.8 4.9 %copy-start.1 = (bf16[224,4096]{1,0:T(8,128)(2,1)S(1)}, bf16[224,4096]{1,0:T(8,128)(2,1)}, u32[]{:S(2)}) copy-start(bf16[224,4096]{1,0:T(8,128)(2,1)} %param.15) | copy-start | bytes 5505028
Sparse Core Ops, SparseCore 0:
  19.1 48.5 all-gather.2
  116.5 89.9 reduce-scatter.1
  234.4 42.2 all-gather.4
